TPU v7x, 32 devices: a whole 2x2x4 slice. The times are simulated.
32 devices in a mesh: groups: 2 (over x), tensor: 8 (over z, y), req: 2 (over core).
Axes of the slice: x: 2, y: 2, z: 4, core: 2. Of those that a mesh axis runs over, the one named last changes fastest.
Arguments:
- queries: bfloat16 [32, 64, 128], P(('groups', 'req'), 'tensor'), parts along dimension 0, may hold values from -48 to 48
- key_cache: bfloat16 [32, 4096, 4, 128], P(('groups', 'req'), 'tensor'), parts along dimension 0, may hold values from -16 to 16
- value_cache: bfloat16 [32, 4096, 4, 128], P(('groups', 'req'), 'tensor'), parts along dimension 0, may hold values from -6 to 6
- fresh_pair: bfloat16 [32, 2, 4, 128], P(('groups', 'req')), parts along dimension 0, may hold values from -12 to 12
- lengths: int32 [32], P(('groups', 'req')), parts along dimension 0, may hold values from 256 to 4096, as said below
- out_weight: bfloat16 [8192, 16384], P('tensor'), may hold values from -0.09375 to 0.09375
- residual: bfloat16 [32, 16384], P(('groups', 'req'), 'tensor'), parts along dimension 0, may hold values from -40 to 40
- norm_gain: bfloat16 [16384], replicated, may hold values from 0.5 to 1.5
- partial_exponents: int32 [8, 32, 128], P('tensor', ('groups', 'req')), parts along dimension 1, may hold values from -13 to -9
- normed_exponents: int32 [32, 128], P(('groups', 'req')), parts along dimension 0, may hold values from -8 to -5
Outputs:
- hidden_state: bfloat16 [32, 16384], P(('groups', 'req'), 'tensor'), parts along dimension 0
- normed: bfloat16 [32, 16384], P(('groups', 'req')), parts along dimension 0
There are 2 independent parts, one for each index of `groups`. A program takes and returns all parts, laid end to end along the dimension named above; an argument that names none is the same for every part. Nothing has to cross between parts.
Inputs may be any that keep to these rules, and one draw needn't show every extreme that they name: Row r holds keys at cache positions below lengths[r]; some row of each draw has all 4096.
All inputs are finite; a program needn't handle non-finite values.
Results may differ from a plain program's by a relative error of at most 0.0075.
Values may be sent and summed in bfloat16 or wider, within the bound.
A program may use at most 192 MiB of HBM per device.

v0:
```python
import functools
import math

import jax
import jax.numpy as jnp
from jax import lax
from jax.experimental import pallas as pl
from jax.experimental.pallas import tpu as pltpu
from jax.sharding import PartitionSpec as P

MESH = pl.DeviceIdType.MESH
LOW = -1e30


def power_two(exponents):
    shifted = exponents + 32
    result = jnp.full(exponents.shape, 2.0**-32, jnp.float32)
    for bit in range(6):
        is_set = (lax.shift_right_logical(shifted, bit) & 1) == 1
        result = result * jnp.where(is_set, jnp.float32(2.0 ** (2**bit)), jnp.float32(1.0))
    return result


def kernel(
    n,
    own_heads,
    kv_count,
    lengths_ref,
    q_hbm,
    k_hbm,
    v_hbm,
    fresh_hbm,
    w_hbm,
    residual_hbm,
    gain_hbm,
    pexp_hbm,
    nexp_hbm,
    hidden_ref,
    normed_ref,
    kbuf,
    vbuf,
    wbuf,
    qbuf,
    q32,
    fresh,
    residual,
    gain,
    pexp,
    nexp,
    groups_at,
    plim,
    nlim,
    mix32,
    mix_out,
    mix_in,
    stat_own,
    stat_in,
    att,
    rs_out,
    rs_in,
    ag,
    k_sem,
    v_sem,
    w_sem,
    small_sem,
    own_sem,
    send_sem,
    recv_sem,
):
    me = lax.axis_index("tensor")
    rows = kbuf.shape[0]
    spots = kbuf.shape[1]
    head_size = kbuf.shape[2]
    heads = n * own_heads
    per_group = heads // kv_count
    share = wbuf.shape[2]
    half = share // 2
    block = 128
    blocks = share // block
    c = head_size ** (-0.5) / math.log(2.0)

    def partner(k):
        return lax.rem(me + k, n)

    barrier = pltpu.get_barrier_semaphore()

    @pl.loop(1, n)
    def _(k):
        pl.semaphore_signal(barrier, inc=1, device_id={"tensor": partner(k)}, device_id_type=MESH)

    own_q = pltpu.make_async_copy(q_hbm, qbuf.at[me], own_sem)
    own_q.start()
    small = [
        pltpu.make_async_copy(fresh_hbm, fresh, small_sem.at[0]),
        pltpu.make_async_copy(pexp_hbm, pexp, small_sem.at[1]),
        pltpu.make_async_copy(nexp_hbm, nexp, small_sem.at[2]),
        pltpu.make_async_copy(gain_hbm, gain, small_sem.at[3]),
        pltpu.make_async_copy(residual_hbm, residual, small_sem.at[4]),
    ]
    for copy in small:
        copy.start()

    def k_copy(r):
        return pltpu.make_async_copy(k_hbm.at[r], kbuf.at[r], k_sem.at[r])

    def v_copy(r):
        return pltpu.make_async_copy(v_hbm.at[r], vbuf.at[r], v_sem.at[r])

    def w_copy(j):
        return pltpu.make_async_copy(
            w_hbm.at[:, pl.ds(pl.multiple_of(j * share, share), share)], wbuf.at[j], w_sem.at[j]
        )

    for r in range(rows):
        k_copy(r).start()
        v_copy(r).start()

    @pl.loop(0, n)
    def _(k):
        w_copy(partner(k + 1)).start()

    own_q.wait()
    pl.semaphore_wait(barrier, n - 1)

    def remote(phase, src, dst, to, frm):
        return pltpu.make_async_remote_copy(
            src_ref=src,
            dst_ref=dst,
            send_sem=send_sem.at[phase, to],
            recv_sem=recv_sem.at[phase, frm],
            device_id={"tensor": to},
            device_id_type=MESH,
        )

    @pl.loop(1, n)
    def _(k):
        remote(0, qbuf.at[me], qbuf.at[me], partner(k), me).start()

    columns = lax.broadcasted_iota(jnp.int32, (heads, spots), 1)
    head_of = lax.broadcasted_iota(jnp.int32, (heads, spots), 0)
    groups_at[...] = jnp.where(
        lax.rem(columns, kv_count) == lax.div(head_of, per_group), columns, 1 << 24
    )
    for copy in small:
        copy.wait()
    plimits = 448.0 * power_two(pexp[0])
    nlimits = 448.0 * power_two(nexp[...])
    for b in range(n * blocks):
        plim[b] = jnp.broadcast_to(plimits[:, b : b + 1], (rows, block))
        nlim[b] = jnp.broadcast_to(nlimits[:, b : b + 1], (rows, block))

    @pl.loop(1, n)
    def _(k):
        src = partner(k)
        remote(0, qbuf.at[src], qbuf.at[src], src, src).wait_recv()

    for t in range(n):
        q32[:, t * own_heads : (t + 1) * own_heads, :] = (
            qbuf[t].astype(jnp.float32).reshape(rows, own_heads, head_size)
        )

    @pl.loop(0, rows)
    def _(r):
        q = q32[r]
        fresh_row = fresh[r].astype(jnp.float32)
        fresh_key = jnp.concatenate(
            [
                jnp.broadcast_to(fresh_row[g : g + 1], (per_group, head_size))
                for g in range(kv_count)
            ],
            axis=0,
        )
        fresh_value = jnp.concatenate(
            [
                jnp.broadcast_to(fresh_row[kv_count + g : kv_count + g + 1], (per_group, head_size))
                for g in range(kv_count)
            ],
            axis=0,
        )
        fresh_score = jnp.sum(q * fresh_key, axis=1, keepdims=True)
        fresh_score = jnp.where(me == 0, fresh_score, LOW)
        k_copy(r).wait()
        scores = lax.dot_general(
            q.astype(jnp.bfloat16),
            kbuf[r],
            (((1,), (1,)), ((), ())),
            preferred_element_type=jnp.float32,
        )
        limit = lengths_ref[r] * kv_count - me * spots
        scores = jnp.where(groups_at[...] < limit, scores, LOW)
        top = jnp.maximum(jnp.max(scores, axis=1, keepdims=True), fresh_score)
        weights = jnp.exp2((scores - top) * c)
        own_weight = jnp.exp2((fresh_score - top) * c)
        total = jnp.sum(weights, axis=1, keepdims=True) + own_weight
        v_copy(r).wait()
        mix = jnp.dot(
            weights.astype(jnp.bfloat16), vbuf[r], preferred_element_type=jnp.float32
        )
        mix = mix + own_weight * fresh_value
        mix32[pl.ds(r, heads, stride=rows), :] = mix
        stats = jnp.concatenate(
            [
                jnp.broadcast_to(top, (heads, 2 * heads)),
                jnp.broadcast_to(total, (heads, 2 * heads)),
            ],
            axis=0,
        )
        stat_own[pl.ds(r, 1), :] = jnp.transpose(stats)[0:1]

    piece = own_heads * rows
    for t in range(n):
        mix_out[t] = mix32[t * piece : (t + 1) * piece, :].astype(jnp.bfloat16)

    @pl.loop(1, n)
    def _(k):
        dst = partner(k)
        remote(2, stat_own, stat_in.at[me], dst, me).start()
        remote(1, mix_out.at[dst], mix_in.at[me], dst, me).start()

    stat_in[me] = stat_own[...]
    mix_in[me] = mix_out[me]

    @pl.loop(1, n)
    def _(k):
        src = partner(k)
        remote(2, stat_own, stat_in.at[src], src, src).wait_recv()
        remote(1, mix_out.at[src], mix_in.at[src], src, src).wait_recv()

    tops = [stat_in[s] for s in range(n)]
    highest = functools.reduce(jnp.maximum, tops)
    scales = [jnp.exp2((top - highest) * c) for top in tops]
    weight_sum = sum(
        pltpu.roll(tops[s], heads, 1) * scales[s] for s in range(n)
    )
    shift = lax.rem(2 * heads - me * own_heads, 2 * heads)
    inverse = 1.0 / weight_sum
    scales = [pltpu.roll(scale * inverse, shift, 1) for scale in scales]
    arrived = [mix_in[s].astype(jnp.float32) for s in range(n)]
    pieces = []
    for h in range(own_heads):
        pieces.append(
            sum(
                arrived[s][h * rows : (h + 1) * rows] * scales[s][:, h : h + 1] for s in range(n)
            )
        )
    att[...] = jnp.concatenate(pieces, axis=1).astype(jnp.bfloat16)

    step = min(512, half)

    def project(j):
        w_copy(j).wait()
        out = []
        for at in range(0, share, step):
            value = jnp.dot(
                att[...], wbuf[j, :, at : at + step], preferred_element_type=jnp.float32
            )
            limit = jnp.concatenate(
                [plim[j * blocks + at // block + b] for b in range(step // block)], axis=1
            )
            out.append(jnp.clip(value, -limit, limit))
        left = jnp.concatenate(out[: len(out) // 2], axis=1)
        right = jnp.concatenate(out[len(out) // 2 :], axis=1)
        return jnp.concatenate([left, right], axis=0).astype(jnp.bfloat16)

    @pl.loop(1, n)
    def _(k):
        dst = partner(k)
        rs_out[dst] = project(dst)
        remote(3, rs_out.at[dst], rs_in.at[me], dst, me).start()

    rs_in[me] = project(me)
    own = residual[...].astype(jnp.float32)
    total = jnp.concatenate([own[:, :half], own[:, half:]], axis=0)

    @pl.loop(1, n)
    def _(k):
        src = partner(k)
        remote(3, rs_out.at[src], rs_in.at[src], src, src).wait_recv()

    summed = rs_in[0].astype(jnp.float32)
    for s in range(1, n):
        summed = summed + rs_in[s].astype(jnp.float32)
    ag[me] = (total + summed).astype(jnp.bfloat16)

    @pl.loop(1, n)
    def _(k):
        remote(4, ag.at[me], ag.at[me], partner(k), me).start()

    state = ag[me].astype(jnp.float32)
    hidden_ref[...] = jnp.concatenate([state[:rows], state[rows:]], axis=1).astype(jnp.bfloat16)

    @pl.loop(1, n)
    def _(k):
        src = partner(k)
        remote(4, ag.at[src], ag.at[src], src, src).wait_recv()

    squares = jnp.zeros((2 * rows, half), jnp.float32)
    for s in range(n):
        value = ag[s].astype(jnp.float32)
        squares = squares + value * value
    squares = jnp.sum(squares, axis=1, keepdims=True)
    squares = squares[:rows] + squares[rows:]
    gains = gain[...].astype(jnp.float32)
    root = lax.rsqrt(squares / (n * share) + 1e-05)
    for s in range(n):
        value = ag[s].astype(jnp.float32)
        out = []
        for b in range(blocks):
            side, at = divmod(b * block, half)
            part = value[side * rows : (side + 1) * rows, at : at + block]
            index = s * blocks + b
            scaled = part * root * gains[index : index + 1, :]
            out.append(jnp.clip(scaled, -nlim[index], nlim[index]))
        normed_ref[:, s * share : (s + 1) * share] = jnp.concatenate(out, axis=1).astype(
            jnp.bfloat16
        )

    @pl.loop(1, n)
    def _(k):
        dst = partner(k)
        remote(0, qbuf.at[me], qbuf.at[me], dst, me).wait_send()
        remote(1, mix_out.at[dst], mix_in.at[me], dst, me).wait_send()
        remote(2, stat_own, stat_in.at[me], dst, me).wait_send()
        remote(3, rs_out.at[dst], rs_in.at[me], dst, me).wait_send()
        remote(4, ag.at[me], ag.at[me], dst, me).wait_send()


def on_device(
    n,
    queries,
    key_cache,
    value_cache,
    fresh_pair,
    lengths,
    out_weight,
    residual,
    norm_gain,
    partial_exponents,
    normed_exponents,
):
    rows, own_heads, head_size = queries.shape
    positions, kv_count = key_cache.shape[1:3]
    spots = positions * kv_count
    heads = n * own_heads
    depth, width = out_weight.shape
    share = width // n
    half = share // 2
    all_blocks = normed_exponents.shape[1]
    block = width // all_blocks
    piece = rows * own_heads
    anywhere = pl.BlockSpec(memory_space=pl.ANY)
    in_vmem = pl.BlockSpec(memory_space=pltpu.VMEM)
    bf16, f32 = jnp.bfloat16, jnp.float32
    dma = pltpu.SemaphoreType.DMA
    return pl.pallas_call(
        functools.partial(kernel, n, own_heads, kv_count),
        out_shape=(
            jax.ShapeDtypeStruct((rows, share), bf16),
            jax.ShapeDtypeStruct((rows, width), bf16),
        ),
        in_specs=[pl.BlockSpec(memory_space=pltpu.SMEM)] + [anywhere] * 9,
        out_specs=(in_vmem, in_vmem),
        scratch_shapes=[
            pltpu.VMEM((rows, spots, head_size), bf16),
            pltpu.VMEM((rows, spots, head_size), bf16),
            pltpu.VMEM((n, depth, share), bf16),
            pltpu.VMEM((n, piece, head_size), bf16),
            pltpu.VMEM((rows, heads, head_size), f32),
            pltpu.VMEM((rows, 2 * kv_count, head_size), bf16),
            pltpu.VMEM((rows, share), bf16),
            pltpu.VMEM((all_blocks, block), bf16),
            pltpu.VMEM((1, rows, all_blocks), jnp.int32),
            pltpu.VMEM((rows, all_blocks), jnp.int32),
            pltpu.VMEM((heads, spots), jnp.int32),
            pltpu.VMEM((all_blocks, rows, block), f32),
            pltpu.VMEM((all_blocks, rows, block), f32),
            pltpu.VMEM((heads * rows, head_size), f32),
            pltpu.VMEM((n, piece, head_size), bf16),
            pltpu.VMEM((n, piece, head_size), bf16),
            pltpu.VMEM((rows, 2 * heads), f32),
            pltpu.VMEM((n, rows, 2 * heads), f32),
            pltpu.VMEM((rows, depth), bf16),
            pltpu.VMEM((n, 2 * rows, half), bf16),
            pltpu.VMEM((n, 2 * rows, half), bf16),
            pltpu.VMEM((n, 2 * rows, half), bf16),
            dma((rows,)),
            dma((rows,)),
            dma((n,)),
            dma((5,)),
            dma,
            dma((5, n)),
            dma((5, n)),
        ],
        compiler_params=pltpu.CompilerParams(
            collective_id=0, has_side_effects=True, vmem_limit_bytes=60 * 2**20
        ),
    )(
        lengths,
        queries.reshape(piece, head_size),
        key_cache.reshape(rows, spots, head_size),
        value_cache.reshape(rows, spots, head_size),
        fresh_pair.reshape(rows, 2 * kv_count, head_size),
        out_weight,
        residual,
        norm_gain.reshape(all_blocks, block),
        partial_exponents,
        normed_exponents,
    )


def solution(mesh):
    return jax.shard_map(
        functools.partial(on_device, mesh.shape["tensor"]),
        mesh=mesh,
        in_specs=(
            P(("groups", "req"), "tensor", None),
            P(("groups", "req"), "tensor", None, None),
            P(("groups", "req"), "tensor", None, None),
            P(("groups", "req"), None, None, None),
            P(("groups", "req")),
            P("tensor", None),
            P(("groups", "req"), "tensor"),
            P(),
            P("tensor", ("groups", "req"), None),
            P(("groups", "req"), None),
        ),
        out_specs=(P(("groups", "req"), "tensor"), P(("groups", "req"), None)),
        check_vma=False,
    )
```

profile of v0, /device:TPU:0, one launch (start us, length us, event | category | flops | bytes accessed | tf_op | source)
XLA Modules:
  0.0 43.0 jit_solution(17879233312843772549)
XLA Ops:
  0.6 39.3 %shard_map.113 = (bf16[8,2048]{1,0:T(8,128)(2,1)}, bf16[8,16384]{1,0:T(8,128)(2,1)}) custom-call(s32[8]{0:T(128)} %lengths_ref.1, bf16[64,128]{1,0:T(8,128)(2,1)} %bitcast.8, bf16[8,2048,128]{2,1,0:T(8,128)(2,1)} %bitcast.5, bf16[8,2048,128]{2,1,0:T(8,128)(2,1)} %bitcast.6, bf16[8,8,128]{2,1,0:T(8,128)(2,1)} %bitcast.9, bf16[1024,16384]{1,0:T(8,128)(2,1)} %w_hbm.1, ...), custom_call_target="tpu_custom_call" | custom-call | tf_op jit(solution)/shard_map/pallas_call | solution.py:355
  39.9 1.4 %copy.14 = bf16[8,2048]{1,0:T(8,128)(2,1)} copy(bf16[8,2048]{1,0:T(8,128)(2,1)} %get-tuple-element.4) | data formatting | bytes 65536
  41.3 1.7 %copy.15 = bf16[8,16384]{1,0:T(8,128)(2,1)} copy(bf16[8,16384]{1,0:T(8,128)(2,1)} %get-tuple-element.5) | data formatting | bytes 524288
where the time goes:
time: 43.2 us; the launch traced here: 43 us
  Pallas kernels  39.3 us (91%)
  local copies, waits for them, and re-layouts  3.04 us (7%)
  between operations  0.64 us (1%)
    pallas_call x1, Pallas kernels, on_device(): pl.pallas_call(functools.partial(kernel, n, own_heads, kv_count), out_sha...  39.3 us
    unnamed x2, local copies, waits for them, and re-layouts  3.04 us

commit v1 on v0

--- a/solution.py
+++ b/solution.py
@@ -32,11 +32,8 @@
     fresh_hbm,
     w_hbm,
     residual_hbm,
-    gain_hbm,
     pexp_hbm,
-    nexp_hbm,
-    hidden_ref,
-    normed_ref,
+    ag,
     kbuf,
     vbuf,
     wbuf,
@@ -44,12 +41,9 @@
     q32,
     fresh,
     residual,
-    gain,
     pexp,
-    nexp,
     groups_at,
     plim,
-    nlim,
     mix32,
     mix_out,
     mix_in,
@@ -58,7 +52,7 @@
     att,
     rs_out,
     rs_in,
-    ag,
+    state,
     k_sem,
     v_sem,
     w_sem,
@@ -93,9 +87,7 @@
     small = [
         pltpu.make_async_copy(fresh_hbm, fresh, small_sem.at[0]),
         pltpu.make_async_copy(pexp_hbm, pexp, small_sem.at[1]),
-        pltpu.make_async_copy(nexp_hbm, nexp, small_sem.at[2]),
-        pltpu.make_async_copy(gain_hbm, gain, small_sem.at[3]),
-        pltpu.make_async_copy(residual_hbm, residual, small_sem.at[4]),
+        pltpu.make_async_copy(residual_hbm, residual, small_sem.at[2]),
     ]
     for copy in small:
         copy.start()
@@ -139,15 +131,13 @@
     columns = lax.broadcasted_iota(jnp.int32, (heads, spots), 1)
     head_of = lax.broadcasted_iota(jnp.int32, (heads, spots), 0)
     groups_at[...] = jnp.where(
-        lax.rem(columns, kv_count) == lax.div(head_of, per_group), columns, 1 << 24
+        (columns & (kv_count - 1)) == lax.shift_right_logical(head_of, per_group.bit_length() - 1), columns, 1 << 24
     )
     for copy in small:
         copy.wait()
     plimits = 448.0 * power_two(pexp[0])
-    nlimits = 448.0 * power_two(nexp[...])
     for b in range(n * blocks):
         plim[b] = jnp.broadcast_to(plimits[:, b : b + 1], (rows, block))
-        nlim[b] = jnp.broadcast_to(nlimits[:, b : b + 1], (rows, block))
 
     @pl.loop(1, n)
     def _(k):
@@ -159,45 +149,43 @@
             qbuf[t].astype(jnp.float32).reshape(rows, own_heads, head_size)
         )
 
-    @pl.loop(0, rows)
-    def _(r):
-        q = q32[r]
-        fresh_row = fresh[r].astype(jnp.float32)
-        fresh_key = jnp.concatenate(
+    for r in range(rows):
+        k_copy(r).wait()
+        v_copy(r).wait()
+
+    def score(r):
+        return lax.dot_general(
+            q32[r].astype(jnp.bfloat16),
+            kbuf[r],
+            (((1,), (1,)), ((), ())),
+            preferred_element_type=jnp.float32,
+        )
+
+    def per_head(fresh_row, first):
+        return jnp.concatenate(
             [
-                jnp.broadcast_to(fresh_row[g : g + 1], (per_group, head_size))
+                jnp.broadcast_to(fresh_row[first + g : first + g + 1], (per_group, head_size))
                 for g in range(kv_count)
             ],
             axis=0,
         )
-        fresh_value = jnp.concatenate(
-            [
-                jnp.broadcast_to(fresh_row[kv_count + g : kv_count + g + 1], (per_group, head_size))
-                for g in range(kv_count)
-            ],
-            axis=0,
-        )
-        fresh_score = jnp.sum(q * fresh_key, axis=1, keepdims=True)
+
+    scores = score(0)
+    for r in range(rows):
+        later = score(r + 1) if r + 1 < rows else None
+        fresh_row = fresh[r].astype(jnp.float32)
+        fresh_score = jnp.sum(q32[r] * per_head(fresh_row, 0), axis=1, keepdims=True)
         fresh_score = jnp.where(me == 0, fresh_score, LOW)
-        k_copy(r).wait()
-        scores = lax.dot_general(
-            q.astype(jnp.bfloat16),
-            kbuf[r],
-            (((1,), (1,)), ((), ())),
-            preferred_element_type=jnp.float32,
-        )
         limit = lengths_ref[r] * kv_count - me * spots
         scores = jnp.where(groups_at[...] < limit, scores, LOW)
         top = jnp.maximum(jnp.max(scores, axis=1, keepdims=True), fresh_score)
         weights = jnp.exp2((scores - top) * c)
         own_weight = jnp.exp2((fresh_score - top) * c)
         total = jnp.sum(weights, axis=1, keepdims=True) + own_weight
-        v_copy(r).wait()
-        mix = jnp.dot(
-            weights.astype(jnp.bfloat16), vbuf[r], preferred_element_type=jnp.float32
-        )
-        mix = mix + own_weight * fresh_value
-        mix32[pl.ds(r, heads, stride=rows), :] = mix
+        mix = jnp.dot(weights.astype(jnp.bfloat16), vbuf[r], preferred_element_type=jnp.float32)
+        mix32[pl.ds(r, heads, stride=rows), :] = mix + own_weight * per_head(
+            fresh_row, kv_count
+        )
         stats = jnp.concatenate(
             [
                 jnp.broadcast_to(top, (heads, 2 * heads)),
@@ -206,6 +194,7 @@
             axis=0,
         )
         stat_own[pl.ds(r, 1), :] = jnp.transpose(stats)[0:1]
+        scores = later
 
     piece = own_heads * rows
     for t in range(n):
@@ -280,28 +269,49 @@
     summed = rs_in[0].astype(jnp.float32)
     for s in range(1, n):
         summed = summed + rs_in[s].astype(jnp.float32)
-    ag[me] = (total + summed).astype(jnp.bfloat16)
-
-    @pl.loop(1, n)
-    def _(k):
-        remote(4, ag.at[me], ag.at[me], partner(k), me).start()
-
-    state = ag[me].astype(jnp.float32)
-    hidden_ref[...] = jnp.concatenate([state[:rows], state[rows:]], axis=1).astype(jnp.bfloat16)
+    state[...] = (total + summed).astype(jnp.bfloat16)
+
+    @pl.loop(1, n)
+    def _(k):
+        remote(4, state, ag.at[me], partner(k), me).start()
+
+    own_state = pltpu.make_async_copy(state, ag.at[me], own_sem)
+    own_state.start()
 
     @pl.loop(1, n)
     def _(k):
         src = partner(k)
-        remote(4, ag.at[src], ag.at[src], src, src).wait_recv()
-
+        remote(4, state, ag.at[src], src, src).wait_recv()
+
+    own_state.wait()
+
+    @pl.loop(1, n)
+    def _(k):
+        dst = partner(k)
+        remote(0, qbuf.at[me], qbuf.at[me], dst, me).wait_send()
+        remote(1, mix_out.at[dst], mix_in.at[me], dst, me).wait_send()
+        remote(2, stat_own, stat_in.at[me], dst, me).wait_send()
+        remote(3, rs_out.at[dst], rs_in.at[me], dst, me).wait_send()
+        remote(4, state, ag.at[me], dst, me).wait_send()
+
+
+def norm_kernel(n, gain, nexp, ag, hidden_ref, normed_ref):
+    rows = nexp.shape[0]
+    half = ag.shape[2]
+    share = 2 * half
+    block = gain.shape[1]
+    blocks = share // block
+    own = ag[lax.axis_index("tensor")].astype(jnp.float32)
+    hidden_ref[...] = jnp.concatenate([own[:rows], own[rows:]], axis=1).astype(jnp.bfloat16)
     squares = jnp.zeros((2 * rows, half), jnp.float32)
     for s in range(n):
         value = ag[s].astype(jnp.float32)
         squares = squares + value * value
     squares = jnp.sum(squares, axis=1, keepdims=True)
     squares = squares[:rows] + squares[rows:]
+    root = lax.rsqrt(squares / (n * share) + 1e-05)
+    limits = 448.0 * power_two(nexp[...])
     gains = gain[...].astype(jnp.float32)
-    root = lax.rsqrt(squares / (n * share) + 1e-05)
     for s in range(n):
         value = ag[s].astype(jnp.float32)
         out = []
@@ -310,19 +320,11 @@
             part = value[side * rows : (side + 1) * rows, at : at + block]
             index = s * blocks + b
             scaled = part * root * gains[index : index + 1, :]
-            out.append(jnp.clip(scaled, -nlim[index], nlim[index]))
+            limit = limits[:, index : index + 1]
+            out.append(jnp.clip(scaled, -limit, limit))
         normed_ref[:, s * share : (s + 1) * share] = jnp.concatenate(out, axis=1).astype(
             jnp.bfloat16
         )
-
-    @pl.loop(1, n)
-    def _(k):
-        dst = partner(k)
-        remote(0, qbuf.at[me], qbuf.at[me], dst, me).wait_send()
-        remote(1, mix_out.at[dst], mix_in.at[me], dst, me).wait_send()
-        remote(2, stat_own, stat_in.at[me], dst, me).wait_send()
-        remote(3, rs_out.at[dst], rs_in.at[me], dst, me).wait_send()
-        remote(4, ag.at[me], ag.at[me], dst, me).wait_send()
 
 
 def on_device(
@@ -352,14 +354,11 @@
     in_vmem = pl.BlockSpec(memory_space=pltpu.VMEM)
     bf16, f32 = jnp.bfloat16, jnp.float32
     dma = pltpu.SemaphoreType.DMA
-    return pl.pallas_call(
+    gathered = pl.pallas_call(
         functools.partial(kernel, n, own_heads, kv_count),
-        out_shape=(
-            jax.ShapeDtypeStruct((rows, share), bf16),
-            jax.ShapeDtypeStruct((rows, width), bf16),
-        ),
-        in_specs=[pl.BlockSpec(memory_space=pltpu.SMEM)] + [anywhere] * 9,
-        out_specs=(in_vmem, in_vmem),
+        out_shape=jax.ShapeDtypeStruct((n, 2 * rows, half), bf16),
+        in_specs=[pl.BlockSpec(memory_space=pltpu.SMEM)] + [anywhere] * 7,
+        out_specs=anywhere,
         scratch_shapes=[
             pltpu.VMEM((rows, spots, head_size), bf16),
             pltpu.VMEM((rows, spots, head_size), bf16),
@@ -368,11 +367,8 @@
             pltpu.VMEM((rows, heads, head_size), f32),
             pltpu.VMEM((rows, 2 * kv_count, head_size), bf16),
             pltpu.VMEM((rows, share), bf16),
-            pltpu.VMEM((all_blocks, block), bf16),
             pltpu.VMEM((1, rows, all_blocks), jnp.int32),
-            pltpu.VMEM((rows, all_blocks), jnp.int32),
             pltpu.VMEM((heads, spots), jnp.int32),
-            pltpu.VMEM((all_blocks, rows, block), f32),
             pltpu.VMEM((all_blocks, rows, block), f32),
             pltpu.VMEM((heads * rows, head_size), f32),
             pltpu.VMEM((n, piece, head_size), bf16),
@@ -382,11 +378,11 @@
             pltpu.VMEM((rows, depth), bf16),
             pltpu.VMEM((n, 2 * rows, half), bf16),
             pltpu.VMEM((n, 2 * rows, half), bf16),
-            pltpu.VMEM((n, 2 * rows, half), bf16),
+            pltpu.VMEM((2 * rows, half), bf16),
             dma((rows,)),
             dma((rows,)),
             dma((n,)),
-            dma((5,)),
+            dma((3,)),
             dma,
             dma((5, n)),
             dma((5, n)),
@@ -402,10 +398,18 @@
         fresh_pair.reshape(rows, 2 * kv_count, head_size),
         out_weight,
         residual,
-        norm_gain.reshape(all_blocks, block),
         partial_exponents,
-        normed_exponents,
     )
+    return pl.pallas_call(
+        functools.partial(norm_kernel, n),
+        out_shape=(
+            jax.ShapeDtypeStruct((rows, share), bf16),
+            jax.ShapeDtypeStruct((rows, width), bf16),
+        ),
+        in_specs=[in_vmem] * 3,
+        out_specs=(in_vmem, in_vmem),
+        compiler_params=pltpu.CompilerParams(vmem_limit_bytes=60 * 2**20),
+    )(norm_gain.reshape(all_blocks, block), normed_exponents, gathered)
 
 
 def solution(mesh):

time: 43.2 us -> 37.1 us (0.86)
  local copies, waits for them, and re-layouts: 3.04 us -> 0 us
  Pallas kernels: 39.3 us -> 36.3 us
    pallas_call x1, Pallas kernels: 39.3 us -> 34.3 us  [on_device(): pl.pallas_call(functools.partial(kernel, n, own_heads, kv_count), out_sha...]
    unnamed x2 -> x0, local copies, waits for them, and re-layouts: 3.04 us -> none
    pallas_call x0 -> x1, Pallas kernels: none -> 2.03 us  [on_device(): pl.pallas_call(functools.partial(norm_kernel, n), out_shape=(jax.ShapeDty...]
where the time goes in v1:
time: 37.1 us; the launch traced here: 37 us
  Pallas kernels  36.3 us (98%)
  between operations  0.64 us (2%)
    pallas_call x1, Pallas kernels, on_device(): pl.pallas_call(functools.partial(kernel, n, own_heads, kv_count), out_sha...  34.3 us
    pallas_call x1, Pallas kernels, on_device(): pl.pallas_call(functools.partial(norm_kernel, n), out_shape=(jax.ShapeDty...  2.03 us

profile of v1, /device:TPU:0, one launch (start us, length us, event | category | flops | bytes accessed | tf_op | source)
XLA Modules:
  0.0 37.0 jit_solution(6948568130754871570)
XLA Ops:
  0.6 34.3 %shard_map.113.ag = bf16[8,16,1024]{2,1,0:T(8,128)(2,1)} custom-call(s32[8]{0:T(128)} %lengths_ref.1, bf16[64,128]{1,0:T(8,128)(2,1)} %bitcast.8, bf16[8,2048,128]{2,1,0:T(8,128)(2,1)} %bitcast.5, bf16[8,2048,128]{2,1,0:T(8,128)(2,1)} %bitcast.6, bf16[8,8,128]{2,1,0:T(8,128)(2,1)} %bitcast.9, bf16[1024,16384]{1,0:T(8,128)(2,1)} %w_hbm.1, ...), custom_call_target="tpu_custom_call" | custom-call | tf_op jit(solution)/shard_map/pallas_call | solution.py:357
  34.9 2.0 %shard_map.114 = (bf16[8,2048]{1,0:T(8,128)(2,1)}, bf16[8,16384]{1,0:T(8,128)(2,1)}) custom-call(bf16[128,128]{1,0:T(8,128)(2,1)} %bitcast.7, s32[8,128]{1,0:T(8,128)} %nexp.1, bf16[8,16,1024]{2,1,0:T(8,128)(2,1)} %shard_map.113.ag), custom_call_target="tpu_custom_call" | custom-call | tf_op jit(solution)/shard_map/pallas_call | solution.py:403

commit v2 on v1

--- a/solution.py
+++ b/solution.py
@@ -73,6 +73,9 @@
     blocks = share // block
     c = head_size ** (-0.5) / math.log(2.0)
 
+    parts = 2 if rows * own_heads % 32 == 0 else 1
+    q_part = rows * own_heads // parts
+
     def partner(k):
         return lax.rem(me + k, n)
 
@@ -124,9 +127,15 @@
             device_id_type=MESH,
         )
 
-    @pl.loop(1, n)
-    def _(k):
-        remote(0, qbuf.at[me], qbuf.at[me], partner(k), me).start()
+    def q_copy(p, to, frm, slot):
+        part = qbuf.at[slot, pl.ds(p * q_part, q_part)]
+        return remote(0 if p == 0 else 5, part, part, to, frm)
+
+    for p in range(parts):
+
+        @pl.loop(1, n)
+        def _(k):
+            q_copy(p, partner(k), me, me).start()
 
     columns = lax.broadcasted_iota(jnp.int32, (heads, spots), 1)
     head_of = lax.broadcasted_iota(jnp.int32, (heads, spots), 0)
@@ -139,19 +148,23 @@
     for b in range(n * blocks):
         plim[b] = jnp.broadcast_to(plimits[:, b : b + 1], (rows, block))
 
-    @pl.loop(1, n)
-    def _(k):
-        src = partner(k)
-        remote(0, qbuf.at[src], qbuf.at[src], src, src).wait_recv()
-
-    for t in range(n):
-        q32[:, t * own_heads : (t + 1) * own_heads, :] = (
-            qbuf[t].astype(jnp.float32).reshape(rows, own_heads, head_size)
-        )
-
     for r in range(rows):
         k_copy(r).wait()
         v_copy(r).wait()
+
+    def take_queries(p):
+        @pl.loop(1, n)
+        def _(k):
+            src = partner(k)
+            q_copy(p, src, src, src).wait_recv()
+
+        count = rows // parts
+        for t in range(n):
+            q32[p * count : (p + 1) * count, t * own_heads : (t + 1) * own_heads, :] = (
+                qbuf[t, p * q_part : (p + 1) * q_part]
+                .astype(jnp.float32)
+                .reshape(count, own_heads, head_size)
+            )
 
     def score(r):
         return lax.dot_general(
@@ -170,9 +183,11 @@
             axis=0,
         )
 
-    scores = score(0)
     for r in range(rows):
-        later = score(r + 1) if r + 1 < rows else None
+        if r % (rows // parts) == 0:
+            take_queries(r * parts // rows)
+            scores = score(r)
+        later = score(r + 1) if (r + 1) % (rows // parts) else None
         fresh_row = fresh[r].astype(jnp.float32)
         fresh_score = jnp.sum(q32[r] * per_head(fresh_row, 0), axis=1, keepdims=True)
         fresh_score = jnp.where(me == 0, fresh_score, LOW)
@@ -288,7 +303,8 @@
     @pl.loop(1, n)
     def _(k):
         dst = partner(k)
-        remote(0, qbuf.at[me], qbuf.at[me], dst, me).wait_send()
+        for p in range(parts):
+            q_copy(p, dst, me, me).wait_send()
         remote(1, mix_out.at[dst], mix_in.at[me], dst, me).wait_send()
         remote(2, stat_own, stat_in.at[me], dst, me).wait_send()
         remote(3, rs_out.at[dst], rs_in.at[me], dst, me).wait_send()
@@ -384,8 +400,8 @@
             dma((n,)),
             dma((3,)),
             dma,
-            dma((5, n)),
-            dma((5, n)),
+            dma((6, n)),
+            dma((6, n)),
         ],
         compiler_params=pltpu.CompilerParams(
             collective_id=0, has_side_effects=True, vmem_limit_bytes=60 * 2**20

time: 37.1 us -> 36.3 us (0.978)
  Pallas kernels: 36.3 us -> 35.5 us
    pallas_call x1, Pallas kernels: 34.3 us -> 33.5 us  [on_device(): pl.pallas_call(functools.partial(kernel, n, own_heads, kv_count), out_sha...]
where the time goes in v2:
time: 36.3 us; the launch traced here: 36.1 us
  Pallas kernels  35.5 us (98%)
  between operations  0.64 us (2%)
    pallas_call x1, Pallas kernels, on_device(): pl.pallas_call(functools.partial(kernel, n, own_heads, kv_count), out_sha...  33.5 us
    pallas_call x1, Pallas kernels, on_device(): pl.pallas_call(functools.partial(norm_kernel, n), out_shape=(jax.ShapeDty...  2.03 us

profile of v2, /device:TPU:0, one launch (start us, length us, event | category | flops | bytes accessed | tf_op | source)
XLA Modules:
  0.0 36.1 jit_solution(4190961141787221812)
XLA Ops:
  0.6 33.5 %shard_map.113.ag = bf16[8,16,1024]{2,1,0:T(8,128)(2,1)} custom-call(s32[8]{0:T(128)} %lengths_ref.1, bf16[64,128]{1,0:T(8,128)(2,1)} %bitcast.8, bf16[8,2048,128]{2,1,0:T(8,128)(2,1)} %bitcast.5, bf16[8,2048,128]{2,1,0:T(8,128)(2,1)} %bitcast.6, bf16[8,8,128]{2,1,0:T(8,128)(2,1)} %bitcast.9, bf16[1024,16384]{1,0:T(8,128)(2,1)} %w_hbm.1, ...), custom_call_target="tpu_custom_call" | custom-call | tf_op jit(solution)/shard_map/pallas_call | solution.py:373
  34.1 2.0 %shard_map.114 = (bf16[8,2048]{1,0:T(8,128)(2,1)}, bf16[8,16384]{1,0:T(8,128)(2,1)}) custom-call(bf16[128,128]{1,0:T(8,128)(2,1)} %bitcast.7, s32[8,128]{1,0:T(8,128)} %nexp.1, bf16[8,16,1024]{2,1,0:T(8,128)(2,1)} %shard_map.113.ag), custom_call_target="tpu_custom_call" | custom-call | tf_op jit(solution)/shard_map/pallas_call | solution.py:419
